TPU v7x, 32 devices: a whole 2x2x4 slice. The times are simulated.
32 devices in a mesh: row: 4 (over x, core), col: 8 (over z, y).
Axes of the slice: x: 2, y: 2, z: 4, core: 2. Of those that a mesh axis runs over, the one named last changes fastest.
Arguments:
- children: bfloat16 [20480, 10240], P('row', 'col'), may hold values from -6 to 6
- row_maps: int32 [2, 80], replicated, may hold values from 0 to 159, as said below
- col_maps: int32 [2, 80], replicated, may hold values from 0 to 159, as said below
- pairs: int32 [2048, 2], replicated, may hold values from 0 to 159, as said below
- lower_panel: bfloat16 [20480, 1024], P('row', 'col'), may hold values from -6 to 6
- upper_panel: bfloat16 [1024, 20480], P('row', 'col'), may hold values from -0.1875 to 0.1875
Outputs:
- front: float32 [20480, 20480], P('row', 'col')
Inputs may be any that keep to these rules, and one draw needn't show every extreme that they name: Parent tile row r of the front's order is stored at tile row (r % 4) * 40 + r // 4. In the front's order each row of row_maps is increasing, child tile row i going to parent tile row 2 * i or 2 * i + 1. Of the 40 child tile rows b * 40 to b * 40 + 39 of one child, at most 20 map into any one stored block of tile rows a * 40 to a * 40 + 39, and in every such group of rows some block receives 20. Parent tile column r of the front's order is stored at tile column (r % 8) * 20 + r // 8. In the front's order each row of col_maps is increasing, child tile column j going to parent tile column 2 * j or 2 * j + 1. Of the 10 child tile columns b * 10 to b * 10 + 9 of one child, at most 3 map into any one stored block of tile columns a * 20 to a * 20 + 19, and in every such group some block receives 3. `pairs`: no pair is listed twice.
All inputs are finite; a program needn't handle non-finite values.
Results may differ from a plain program's by a relative error of at most 0.0003.
Values may be sent and summed in bfloat16 or wider, within the bound.
A program may use at most 320 MiB of HBM per device.

v0:
```python
import jax
import jax.numpy as jnp
from jax import lax
from jax.sharding import PartitionSpec as P

TILE = 128
C = 10240


def routing(tile_map, per_source, target_width):
    tile_ids = jnp.arange(tile_map.shape[0], dtype=jnp.int32)
    source = tile_ids // per_source
    target = tile_map // target_width
    same = (
        (target[:, None] == target[None, :])
        & (source[:, None] == source[None, :])
        & (tile_ids[None, :] < tile_ids[:, None])
    )
    ranking = jnp.sum(same.astype(jnp.int32), axis=1)
    return (source, target, ranking)


def send_table(source, target, ranking, own_source, per_source, targets, capacity):
    tile_ids = jnp.arange(source.shape[0], dtype=jnp.int32)
    local_ids = tile_ids - own_source * per_source
    hits = (
        (source[None, None, :] == own_source)
        & (target[None, None, :] == jnp.arange(targets, dtype=jnp.int32)[:, None, None])
        & (ranking[None, None, :] == jnp.arange(capacity, dtype=jnp.int32)[None, :, None])
    )
    picked = jnp.sum(jnp.where(hits, local_ids[None, None, :], 0), axis=2)
    valid = jnp.any(hits, axis=2)
    return (picked.reshape(-1), valid.reshape(-1))


def receive_table(tile_map, source, ranking, first, count, capacity):
    wanted = first + jnp.arange(count, dtype=jnp.int32)
    hits = tile_map[None, :] == wanted[:, None]
    found = jnp.any(hits, axis=1)
    slot_source = jnp.sum(jnp.where(hits, source[None, :], 0), axis=1)
    slot_rank = jnp.sum(jnp.where(hits, ranking[None, :], 0), axis=1)
    return (slot_source * capacity + slot_rank, found)


def selector(index, valid, sources):
    onehot = (index[None, :] == jnp.arange(sources, dtype=jnp.int32)[:, None]) & valid[None, :]
    lanes = jnp.arange(TILE, dtype=jnp.int32)
    diagonal = lanes[:, None] == lanes[None, :]
    table = onehot[:, None, :, None] & diagonal[None, :, None, :]
    return table.reshape(sources * TILE, index.shape[0] * TILE).astype(jnp.bfloat16)


def body(children, row_maps, col_maps, pairs, lower_panel, upper_panel):
    row_count = lax.axis_size("row")
    col_count = lax.axis_size("col")
    row_here = lax.axis_index("row")
    col_here = lax.axis_index("col")
    tile_count = C // TILE
    parent_count = 2 * tile_count
    col_per = tile_count // col_count
    row_per = 2 * tile_count // row_count
    parent_rows = parent_count // row_count
    parent_cols = parent_count // col_count
    col_cap = -(-(2 * col_per) // col_count)
    row_cap = 2 * row_per // row_count
    half_rows = row_count // 2
    which_child = row_here // half_rows
    row_block = row_here % half_rows
    own_rows = lax.dynamic_index_in_dim(row_maps, which_child, 0, keepdims=False)
    own_cols = lax.dynamic_index_in_dim(col_maps, which_child, 0, keepdims=False)
    zero_tile = jnp.zeros((), jnp.bfloat16)
    row_source, row_target, row_rank = routing(own_rows, row_per, parent_rows)
    row_pick, row_valid = send_table(
        row_source, row_target, row_rank, row_block, row_per, row_count, row_cap
    )
    col_source, col_target, col_rank = routing(own_cols, col_per, parent_cols)
    col_pick, col_valid = send_table(
        col_source, col_target, col_rank, col_here, col_per, col_count, col_cap
    )
    col_choose = selector(col_pick, col_valid, col_per)
    assembled = jnp.zeros((parent_rows, TILE, parent_cols, TILE), jnp.float32)
    outgoing = jnp.dot(children, col_choose, preferred_element_type=jnp.float32).astype(
        jnp.bfloat16
    )
    arrived = lax.all_to_all(outgoing, "col", split_axis=1, concat_axis=1, tiled=True)
    col_slot, col_found = receive_table(
        own_cols, col_source, col_rank, col_here * parent_cols, parent_cols, col_cap
    )
    col_place = selector(col_slot, col_found, col_count * col_cap)
    strip = jnp.dot(arrived, col_place, preferred_element_type=jnp.float32).astype(jnp.bfloat16)
    picked = jnp.take(strip.reshape(row_per, TILE * parent_cols * TILE), row_pick, axis=0)
    picked = jnp.where(row_valid[:, None], picked, zero_tile)
    outgoing = picked.reshape(row_count, row_cap * TILE, parent_cols * TILE)
    arrived = lax.all_to_all(outgoing, "row", split_axis=0, concat_axis=0, tiled=True)
    arrived = arrived.reshape(row_count * row_cap, TILE * parent_cols * TILE)
    for child_id in range(2):
        kid_source, kid_target, kid_rank = routing(row_maps[child_id], row_per, parent_rows)
        row_slot, row_found = receive_table(
            row_maps[child_id],
            kid_source + child_id * half_rows,
            kid_rank,
            row_here * parent_rows,
            parent_rows,
            row_cap,
        )
        gathered = jnp.take(arrived, row_slot, axis=0)
        gathered = jnp.where(row_found[:, None], gathered.astype(jnp.float32), 0.0)
        assembled = assembled + gathered.reshape(parent_rows, TILE, parent_cols, TILE)
    upper_all = lax.all_gather(upper_panel, "row", axis=0, tiled=True)
    product = jnp.dot(
        lax.all_gather(lower_panel, "col", axis=1, tiled=True),
        upper_all,
        preferred_element_type=jnp.float32,
    )
    row_hit = (
        pairs[:, 0][:, None]
        == row_here * parent_rows + jnp.arange(parent_rows, dtype=jnp.int32)[None, :]
    ).astype(jnp.bfloat16)
    col_hit = (
        pairs[:, 1][:, None]
        == col_here * parent_cols + jnp.arange(parent_cols, dtype=jnp.int32)[None, :]
    ).astype(jnp.bfloat16)
    listed = jnp.dot(row_hit.T, col_hit, preferred_element_type=jnp.float32)
    front = (
        assembled - product.reshape(parent_rows, TILE, parent_cols, TILE) * listed[:, None, :, None]
    )
    return front.reshape(parent_rows * TILE, parent_cols * TILE)


def solution(mesh):
    placed = (P("row", "col"), P(), P(), P(), P("row", "col"), P("row", "col"))
    return jax.shard_map(
        body, mesh=mesh, in_specs=placed, out_specs=P("row", "col"), check_vma=False
    )
```

profile of v0, /device:TPU:25, one launch (start us, length us, event | category | flops | bytes accessed | tf_op | source)
XLA Modules:
  0.0 2212.3 jit_solution(1559895493779979056)
XLA Ops:
  6.5 0.7 and_select_fusion.7
  7.2 0.7 fusion.33
  9.0 2.1 broadcast_and_fusion.1
  11.1 46.6 %convolution_convert_fusion = bf16[3072,5120]{1,0:T(8,128)(2,1)} fusion(bf16[5120,1280]{1,0:T(8,128)(2,1)} %param.8, pred[160,8,24,128]{3,2,1,0:T(8,128)(4,1)S(1)} %bitcast.73), kind=kOutput, calls=%fused_computation.18 | convolution fusion | flops 40284979200 | bytes 48496640 | tf_op jit(solution)/shard_map/dot_general | solution.py:82
  57.7 20.3 all-to-all-start
  78.1 0.6 slice_bitcast_fusion.1
  78.7 0.8 convert_reduce_fusion
  79.5 0.4 fusion.13
  80.3 0.6 copy.36
  80.9 0.4 and_reduce_fusion
  81.6 0.6 copy.37
  82.2 0.6 pad_clamp_fusion.2
  82.8 0.2 compare_reduce_fusion.2
  83.2 7.6 broadcast_and_fusion
  90.8 663.9 %all-to-all-done = bf16[5120,8,384]{0,2,1:T(8,128)(2,1)} async-done(((bf16[5120,8,384]{0,2,1:T(8,128)(2,1)}), bf16[5120,8,384]{0,2,1:T(8,128)(2,1)}, u32[]{:S(2)}, u32[]{:S(2)}) %all-to-all-start) | async-done | bytes 31457312 | tf_op jit(solution)/shard_map/all_to_all | solution.py:85
  754.7 89.6 %fusion.3 = bf16[5120,2560]{1,0:T(8,128)(2,1)} fusion(bf16[5120,3072]{0,1:T(8,128)(2,1)} %bitcast.9, pred[320,8,24,128]{3,2,1,0:T(8,128)(4,1)} %bitcast.72), kind=kOutput, calls=%fused_computation.17 | convolution fusion | flops 80543744000 | bytes 65536000 | tf_op jit(solution)/shard_map/dot_general | solution.py:90
  844.3 35.8 %reshape.525 = bf16[40,327680]{1,0:T(8,128)(2,1)} reshape(bf16[5120,2560]{1,0:T(8,128)(2,1)} %fusion.3) | data formatting | bytes 52428800 | tf_op jit(solution)/shard_map/reshape | solution.py:91
  880.1 11.9 fusion.37
  891.9 7.7 mini-gather-slice.17
  899.6 41.9 %gather_fusion = bf16[80,109312]{1,0:T(8,128)(2,1)} fusion(bf16[40,109312]{1,0:T(8,128)(2,1)} %get-tuple-element.30, s32[1024]{0:T(1024)} %pad_clamp_fusion.2), kind=kCustom, calls=%fused_computation.6 | custom fusion | bytes 34980160 | tf_op jit(solution)/shard_map/jit(_take)/gather | solution.py:91
  941.5 41.6 %gather_fusion.1 = bf16[80,109312]{1,0:T(8,128)(2,1)} fusion(bf16[40,109312]{1,0:T(8,128)(2,1)} %get-tuple-element.31, s32[1024]{0:T(1024)} %pad_clamp_fusion.2), kind=kCustom, calls=%fused_computation.7 | custom fusion | bytes 34980160 | tf_op jit(solution)/shard_map/jit(_take)/gather | solution.py:91
  983.1 41.7 %gather_fusion.2 = bf16[80,109056]{1,0:T(8,128)(2,1)} fusion(bf16[40,109056]{1,0:T(8,128)(2,1)} %mini-gather-slice.17, s32[1024]{0:T(1024)} %pad_clamp_fusion.2), kind=kCustom, calls=%fused_computation.8 | custom fusion | bytes 34898240 | tf_op jit(solution)/shard_map/jit(_take)/gather | solution.py:91
  1024.8 43.0 %pad_maximum_fusion = bf16[80,327680]{1,0:T(8,128)(2,1)} fusion(bf16[80,109056]{1,0:T(8,128)(2,1)} %gather_fusion.2, bf16[80,109312]{1,0:T(8,128)(2,1)} %gather_fusion.1, bf16[80,109312]{1,0:T(8,128)(2,1)} %gather_fusion), kind=kLoop, calls=%fused_computation.10 | loop fusion | flops 157286400 | bytes 104857600
  1067.9 71.6 %gather.10 = bf16[4,2560,2560]{2,1,0:T(8,128)(2,1)} reshape(bf16[80,327680]{1,0:T(8,128)(2,1)} %pad_maximum_fusion) | data formatting | bytes 104857600 | tf_op jit(solution)/shard_map/jit(_take)/gather | solution.py:91
  1139.5 35.2 %select_select_fusion = bf16[4,2560,2560]{2,1,0:T(8,128)(2,1)} fusion(bf16[4,2560,2560]{2,1,0:T(8,128)(2,1)} %gather.10, pred[4,2560]{1,0:T(4,128)(4,1)S(1)} %bitcast.74, pred[4,2560]{1,0:T(4,128)(4,1)S(1)} %bitcast.75), kind=kLoop, calls=%fused_computation.13 | loop fusion | flops 52428800 | bytes 104878080 | tf_op jit(solution)/shard_map/jit(_where)/select_n | solution.py:92
  1174.7 17.3 all-to-all-start.1
  1192.0 0.7 all-gather.5.cloned.1.call-update
  1192.7 0.7 all-gather.3.cloned.1.call-update
  1193.5 1.0 fusion.6
  1194.5 18.1 mul.46
  1212.5 35.6 %copy.35 = f32[320,8,40,128]{3,1,2,0:T(8,128)} copy(f32[320,8,40,128]{3,2,1,0:T(8,128)} %bitcast.69) | data formatting | bytes 104857600
  1248.2 52.4 %copy.16 = f32[5120,2560]{1,0:T(8,128)} copy(f32[5120,2560]{0,1:T(8,128)} %bitcast.70) | data formatting | bytes 104857600 | tf_op jit(solution)/shard_map/mul | solution.py:125
  1300.7 0.2 fusion.20
  1300.9 0.5 compare_and_fusion.4
  1301.5 0.7 compare_reduce_fusion.1
  1302.2 482.1 %all-to-all-done.1 = bf16[4,2560,2560]{2,1,0:T(8,128)(2,1)} async-done(((bf16[4,2560,2560]{2,1,0:T(8,128)(2,1)}), bf16[4,2560,2560]{2,1,0:T(8,128)(2,1)}, u32[]{:S(2)}, u32[]{:S(2)}) %all-to-all-start.1) | async-done | bytes 52428832 | tf_op jit(solution)/shard_map/all_to_all | solution.py:94
  1784.3 72.0 %reshape.527 = bf16[80,327680]{1,0:T(8,128)(2,1)} reshape(bf16[4,2560,2560]{2,1,0:T(8,128)(2,1)} %all-to-all-done.1) | data formatting | bytes 104857600 | tf_op jit(solution)/shard_map/reshape | solution.py:95
  1856.3 25.8 %fusion.36 = (bf16[80,109312]{1,0:T(8,128)(2,1)}, bf16[80,109312]{1,0:T(8,128)(2,1)}) fusion(bf16[80,327680]{1,0:T(8,128)(2,1)} %reshape.527), kind=kLoop, calls=%fused_computation.124 | loop fusion | bytes 69959680 | tf_op jit(solution)/shard_map/jit(_take)/gather | solution.py:106
  1882.2 25.2 %gather_fusion.4 = bf16[40,109312]{1,0:T(8,128)(2,1)} fusion(bf16[80,109312]{1,0:T(8,128)(2,1)} %get-tuple-element.29, s32[1024]{0:T(1024)S(1)} %pad_clamp_fusion.1), kind=kCustom, calls=%fused_computation.1.clone | custom fusion | bytes 17490080 | tf_op jit(solution)/shard_map/jit(_take)/gather | solution.py:106
  1907.3 25.4 %gather_fusion.7 = bf16[40,109312]{1,0:T(8,128)(2,1)} fusion(bf16[80,109312]{1,0:T(8,128)(2,1)} %get-tuple-element.29, s32[1024]{0:T(1024)S(1)} %pad_clamp_fusion), kind=kCustom, calls=%fused_computation.4.clone | custom fusion | bytes 17490080 | tf_op jit(solution)/shard_map/jit(_take)/gather | solution.py:106
  1932.7 25.3 %gather_fusion.6 = bf16[40,109312]{1,0:T(8,128)(2,1)} fusion(bf16[80,109312]{1,0:T(8,128)(2,1)} %get-tuple-element.28, s32[1024]{0:T(1024)S(1)} %pad_clamp_fusion), kind=kCustom, calls=%fused_computation.3.clone | custom fusion | bytes 17490080 | tf_op jit(solution)/shard_map/jit(_take)/gather | solution.py:106
  1958.0 25.7 %gather_fusion.3 = bf16[40,109312]{1,0:T(8,128)(2,1)} fusion(bf16[80,109312]{1,0:T(8,128)(2,1)} %get-tuple-element.28, s32[1024]{0:T(1024)S(1)} %pad_clamp_fusion.1), kind=kCustom, calls=%fused_computation.clone | custom fusion | bytes 17490080 | tf_op jit(solution)/shard_map/jit(_take)/gather | solution.py:106
  1983.7 14.2 mini-gather-slice.20
  1997.8 25.3 %gather_fusion.8 = bf16[40,109056]{1,0:T(8,128)(2,1)} fusion(bf16[80,109056]{1,0:T(8,128)(2,1)} %mini-gather-slice.20, s32[1024]{0:T(1024)S(1)} %pad_clamp_fusion), kind=kCustom, calls=%fused_computation.5.clone | custom fusion | bytes 17449120 | tf_op jit(solution)/shard_map/jit(_take)/gather | solution.py:106
  2023.1 25.1 %gather_fusion.5 = bf16[40,109056]{1,0:T(8,128)(2,1)} fusion(bf16[80,109056]{1,0:T(8,128)(2,1)} %mini-gather-slice.20, s32[1024]{0:T(1024)S(1)} %pad_clamp_fusion.1), kind=kCustom, calls=%fused_computation.2.clone | custom fusion | bytes 17449120 | tf_op jit(solution)/shard_map/jit(_take)/gather | solution.py:106
  2048.3 47.8 %select_add_fusion = f32[40,327680]{1,0:T(8,128)} fusion(bf16[40,109056]{1,0:T(8,128)(2,1)} %gather_fusion.5, bf16[40,109312]{1,0:T(8,128)(2,1)} %gather_fusion.4, bf16[40,109312]{1,0:T(8,128)(2,1)} %gather_fusion.3, bf16[40,109056]{1,0:T(8,128)(2,1)} %gather_fusion.8, bf16[40,109312]{1,0:T(8,128)(2,1)} %gather_fusion.7, ...), kind=kLoop, calls=%fused_computation.12 | loop fusion | flops 249036800 | bytes 104857760 | tf_op jit(solution)/shard_map/add | solution.py:108
  2096.1 48.9 %add.175 = f32[5120,2560]{1,0:T(8,128)} reshape(f32[40,327680]{1,0:T(8,128)} %select_add_fusion) | data formatting | bytes 104857600 | tf_op jit(solution)/shard_map/add | solution.py:108
  2145.0 60.2 %multiply_subtract_fusion = f32[5120,2560]{1,0:T(8,128)} fusion(f32[5120,2560]{1,0:T(8,128)} %add.175, f32[5120,2560]{1,0:T(8,128)} %copy.16, bf16[5120,1024]{1,0:T(8,128)(2,1)} %all-gather.3.cloned.1.call-done, bf16[1024,2560]{1,0:T(8,128)(2,1)} %all-gather.5.cloned.1.call-done), kind=kOutput, calls=%fused_computation.11 | convolution fusion | flops 26869760000 | bytes 173015040 | tf_op jit(solution)/shard_map/dot_general | solution.py:110
  (73 shorter events, 2.1 us)
Async XLA Ops:
  57.7 20.4 copy-start.3
  57.7 697.0 %all-to-all-start = ((bf16[5120,8,384]{0,2,1:T(8,128)(2,1)}), bf16[5120,8,384]{0,2,1:T(8,128)(2,1)}, u32[]{:S(2)}, u32[]{:S(2)}) async-start(bf16[5120,8,384]{0,2,1:T(8,128)(2,1)} %bitcast.71), calls=%async_computation | async-start | bytes 62914560 | tf_op jit(solution)/shard_map/all_to_all | solution.py:85
  78.1 1.5 copy-start.6
  82.2 762.1 %copy-start.14 = (s32[20]{0:T(128)}, s32[20]{0:T(128)S(1)}, u32[]{:S(2)}) copy-start(s32[20]{0:T(128)S(1)} %iota_add_fusion) | copy-start | bytes 244
  1067.9 71.6 %copy-start = (pred[1,4,20,128]{3,1,2,0:T(4,128)(4,1)S(1)}, pred[1,4,20,128]{3,1,2,0:T(4,128)(4,1)}, u32[]{:S(2)}) copy-start(pred[1,4,20,128]{3,1,2,0:T(4,128)(4,1)} %copy.36) | copy-start | bytes 30724
  1067.9 71.6 %copy-start.1 = (pred[1,4,20,128]{3,1,2,0:T(4,128)(4,1)S(1)}, pred[1,4,20,128]{3,1,2,0:T(4,128)(4,1)}, u32[]{:S(2)}) copy-start(pred[1,4,20,128]{3,1,2,0:T(4,128)(4,1)} %copy.37) | copy-start | bytes 30724
  1174.7 18.8 copy-start.2
  1174.7 18.8 copy-start.15
  1174.7 609.6 %all-to-all-start.1 = ((bf16[4,2560,2560]{2,1,0:T(8,128)(2,1)}), bf16[4,2560,2560]{2,1,0:T(8,128)(2,1)}, u32[]{:S(2)}, u32[]{:S(2)}) async-start(bf16[4,2560,2560]{2,1,0:T(8,128)(2,1)} %select_select_fusion), calls=%async_computation.1 | async-start | bytes 104857600 | tf_op jit(solution)/shard_map/all_to_all | solution.py:94
  1192.0 953.1 %all-gather.5.cloned.1.call-start = ((), (), s32[]{:S(2)}) async-start(), calls=%async_computation.3 | async-start | bytes 6553600 | tf_op jit(solution)/shard_map/all_gather | solution.py:109
  1192.7 952.3 %all-gather.3.cloned.1.call-start = ((), (), s32[]{:S(2)}) async-start(), calls=%async_computation.2 | async-start | bytes 11796480 | tf_op jit(solution)/shard_map/all_gather | solution.py:111
  1248.2 52.5 %copy-start.4 = (s32[80]{0:T(128)S(1)}, s32[80]{0:T(128)}, u32[]{:S(2)}) copy-start(s32[80]{0:T(128)} %get-tuple-element.34) | copy-start | bytes 964
  1248.2 52.5 %copy-start.5 = (s32[80]{0:T(128)S(1)}, s32[80]{0:T(128)}, u32[]{:S(2)}) copy-start(s32[80]{0:T(128)} %get-tuple-element.37) | copy-start | bytes 964
  1248.2 52.5 %copy-start.7 = (s32[80]{0:T(128)S(1)}, s32[80]{0:T(128)}, u32[]{:S(2)}) copy-start(s32[80]{0:T(128)} %copy-done.6) | copy-start | bytes 964
  1248.2 52.5 %copy-start.8 = (s32[80]{0:T(128)S(1)}, s32[80]{0:T(128)}, u32[]{:S(2)}) copy-start(s32[80]{0:T(128)} %get-tuple-element.16) | copy-start | bytes 964
  1248.2 52.5 %copy-start.9 = (s32[80]{0:T(128)S(1)}, s32[80]{0:T(128)}, u32[]{:S(2)}) copy-start(s32[80]{0:T(128)} %get-tuple-element.18) | copy-start | bytes 964
  2023.1 25.1 %copy-start.10 = (pred[40]{0:T(512)(128)(4,1)S(1)}, pred[40]{0:T(512)(128)(4,1)}, u32[]{:S(2)}) copy-start(pred[40]{0:T(512)(128)(4,1)} %get-tuple-element.12) | copy-start | bytes 124
  2023.1 25.1 %copy-start.11 = (pred[40]{0:T(512)(128)(4,1)S(1)}, pred[40]{0:T(512)(128)(4,1)}, u32[]{:S(2)}) copy-start(pred[40]{0:T(512)(128)(4,1)} %get-tuple-element.13) | copy-start | bytes 124
  2023.1 25.1 %copy-start.12 = (pred[40]{0:T(512)(128)(4,1)S(1)}, pred[40]{0:T(512)(128)(4,1)}, u32[]{:S(2)}) copy-start(pred[40]{0:T(512)(128)(4,1)} %get-tuple-element.21) | copy-start | bytes 124
  2023.1 25.1 %copy-start.13 = (pred[40]{0:T(512)(128)(4,1)S(1)}, pred[40]{0:T(512)(128)(4,1)}, u32[]{:S(2)}) copy-start(pred[40]{0:T(512)(128)(4,1)} %get-tuple-element.43) | copy-start | bytes 124
Sparse Core Ops, SparseCore 0:
  1194.3 68.9 all-gather.4
  1265.4 148.8 all-gather.2
where the time goes:
time: 2220 us; the launch traced here: 2210 us
  waiting for transfers between devices  1150 us (52%)
  local copies, waits for them, and re-layouts  673 us (30%)
  matrix products  197 us (9%)
  other arithmetic  142 us (6%)
  starting transfers between devices  37.6 us (2%)
    all_to_all x1, waiting for transfers between devices, body(): lax.all_to_all(outgoing, 'col', split_axis=1, concat_axis=1, tiled=True)  664 us
    all_to_all x1, waiting for transfers between devices, body(): lax.all_to_all(outgoing, 'row', split_axis=0, concat_axis=0, tiled=True)  482 us
    gather x6, local copies, waits for them, and re-layouts, body(): jnp.take(strip.reshape(row_per, TILE * parent_cols * TILE), row_pick, axi...  216 us
    gather x8, local copies, waits for them, and re-layouts, body(): gathered = jnp.take(arrived, row_slot, axis=0)  192 us
    dot_general x1, matrix products, body(): jnp.dot(arrived, col_place, preferred_element_type=jnp.float32)  89.6 us
    reshape x1, local copies, waits for them, and re-layouts, body(): arrived = arrived.reshape(row_count * row_cap, TILE * parent_cols * TILE)  72 us
    mul x2, local copies, waits for them, and re-layouts, body(): product.reshape(parent_rows, TILE, parent_cols, TILE)  70.5 us
    dot_general x1, matrix products, body(): jnp.dot(lax.all_gather(lower_panel, 'col', axis=1, tiled=True), upper_all...  60.2 us
  transfers between devices with their start and end apart: 4, of which 2 were waited for; matrix products, arithmetic and copies ran while one was open for 22% of the time, Pallas kernels for 0%

commit v1 on v0

v1 whole, which is shorter than its diff:
```python
import functools

import jax
import jax.numpy as jnp
from jax import lax
from jax.experimental import pallas as pl
from jax.experimental.pallas import tpu as pltpu
from jax.sharding import PartitionSpec as P

TILE = 128
WINDOW = 3
MESH = pl.DeviceIdType.MESH


def lanes(index):
    return pl.ds(pl.multiple_of(index * TILE, TILE), TILE)


def exchange_kernel(
    nx, nq, kc, pc,
    kids, low, up,
    recv, low_all, up_all,
    send1, recv1, send2, recv2, send3, recv3,
    up_s1, up_r1, up_s3, up_r3,
    low_sr, low_sl, low_r1, low_s2, low_r2,
):
    row = lax.axis_index("row")
    col = lax.axis_index("col")
    x, core = row // 2, row % 2
    q, p = col // 2, col % 2
    core_mate = (2 * x + 1 - core, col)
    p_mate = (row, 2 * q + 1 - p)

    barrier = pltpu.get_barrier_semaphore()
    for dx in range(nx):
        for dq in range(nq):
            if dx == 0 and dq == 0:
                continue
            pl.semaphore_signal(
                barrier, inc=1,
                device_id=(2 * lax.rem(x + dx, nx) + core, 2 * lax.rem(q + dq, nq) + p),
                device_id_type=MESH,
            )
    pl.semaphore_signal(barrier, inc=1, device_id=core_mate, device_id_type=MESH)
    pl.semaphore_signal(barrier, inc=1, device_id=p_mate, device_id_type=MESH)
    pl.semaphore_wait(barrier, nx * nq + 1)

    def remote(src, dst, ssem, rsem, device):
        return pltpu.make_async_remote_copy(
            src_ref=src, dst_ref=dst, send_sem=ssem, recv_sem=rsem,
            device_id=device, device_id_type=MESH,
        )

    def column_of(step, source_q):
        return lax.rem(step + source_q, kc)

    def unit1(step, tx):
        kk = column_of(step, q)
        j = col * kc + kk
        tq, s = j % nq, j // nq
        src = kids.at[:, tx, :, lanes(kk)]
        dst = recv.at[row, :, :, lanes(s)]
        here = (tx == x) & (tq == q)

        def far():
            device = (2 * tx + core, 2 * tq + p)
            return remote(src, dst, send1.at[kk, tx], recv1.at[x, s], device)

        def near():
            return pltpu.make_async_copy(src, dst, recv1.at[x, s])

        return here, far, near

    def issue(step):
        def one(dx, carry):
            here, far, near = unit1(step, lax.rem(x + 1 + dx, nx))

            @pl.when(here)
            def _():
                near().start()

            @pl.when(jnp.logical_not(here))
            def _():
                far().start()

            return carry

        lax.fori_loop(0, nx, one, 0)

    def drain(step):
        def one(dx, carry):
            here, far, _ = unit1(step, lax.rem(x + 1 + dx, nx))

            @pl.when(jnp.logical_not(here))
            def _():
                far().wait_send()

            return carry

        lax.fori_loop(0, nx, one, 0)

    def slot(xs, s, c):
        return recv.at[2 * xs + c, :, :, lanes(s)]

    def pair_copy(xs, s):
        ref = slot(xs, s, core)
        return remote(ref, ref, send2.at[xs, s], recv2.at[xs, s], p_mate)

    def core_copy(xs, s):
        ref = slot(xs, s, core)
        return remote(ref, ref, send3.at[xs, s], recv3.at[xs, s], core_mate)

    def arrivals(step, side, handle):
        def by_q(dq, carry):
            qs = lax.rem(q + dq, nq)
            j = (2 * qs + side) * kc + column_of(step, qs)

            @pl.when(j % nq == q)
            def _():
                lax.fori_loop(0, nx, lambda xs, c: (handle(xs, j // nq), c)[1], 0)

            return carry

        lax.fori_loop(0, nq, by_q, 0)

    def from_source(xs, s):
        ref = slot(xs, s, core)
        pltpu.make_async_copy(ref, ref, recv1.at[xs, s]).wait()
        pair_copy(xs, s).start()
        core_copy(xs, s).start()

    def from_pair(xs, s):
        pair_copy(xs, s).wait_recv()
        core_copy(xs, s).start()

    def up_far(tx):
        return remote(up, up_all.at[row], up_s1.at[tx], up_r1.at[x], (2 * tx + core, col))

    def up_core(xs):
        ref = up_all.at[2 * xs + core]
        return remote(ref, ref, up_s3.at[xs], up_r3.at[xs], core_mate)

    def low_slot(qs, side):
        if len(low_all.shape) == 3:
            return low_all.at[2 * qs + side]
        return low_all.at[:, lanes(2 * qs + side)]

    def low_step(qs, sems, to):
        ref = low_slot(qs, p)
        return remote(ref, ref, sems.at[qs], low_r1.at[qs], (row, 2 * to + p))

    def low_pair(qs):
        ref = low_slot(qs, p)
        return remote(ref, ref, low_s2.at[qs], low_r2.at[qs], p_mate)

    def goes_right(qs):
        return (qs <= q) & (q + 1 < nq)

    def goes_left(qs):
        return (qs >= q) & (q > 0)

    def low_arrived(qs):
        ref = low_slot(qs, p)
        pltpu.make_async_copy(ref, ref, low_r1.at[qs]).wait()

        @pl.when(goes_right(qs))
        def _():
            low_step(qs, low_sr, q + 1).start()

        @pl.when(goes_left(qs))
        def _():
            low_step(qs, low_sl, q - 1).start()

        low_pair(qs).start()

    def up_arrived(xs):
        ref = up_all.at[2 * xs + core]
        pltpu.make_async_copy(ref, ref, up_r1.at[xs]).wait()
        up_core(xs).start()

    pltpu.make_async_copy(low, low_slot(q, p), low_r1.at[q]).start()
    pltpu.make_async_copy(up, up_all.at[row], up_r1.at[x]).start()
    for dx in range(1, nx):
        up_far(lax.rem(x + dx, nx)).start()
    for step in range(min(WINDOW, kc)):
        issue(step)

    def main(m, carry):
        @pl.when(m < nx)
        def _():
            up_arrived(lax.rem(x + m, nx))

        @pl.when((m < nq) & (q - m >= 0))
        def _():
            low_arrived(q - m)

        @pl.when((m > 0) & (q + m < nq))
        def _():
            low_arrived(q + m)

        @pl.when(m < kc)
        def _():
            drain(m)

            @pl.when(m + WINDOW < kc)
            def _():
                issue(m + WINDOW)

            arrivals(m, p, from_source)

        @pl.when((m >= 1) & (m < kc + 1))
        def _():
            arrivals(m - 1, 1 - p, from_pair)

        return carry

    lax.fori_loop(0, max(kc + 1, nq, nx), main, 0)

    def finish_x(xs, carry):
        up_core(xs).wait()

        @pl.when(xs != x)
        def _():
            up_far(xs).wait_send()

        def finish_s(s, inner):
            j = s * nq + q

            @pl.when((j // kc) % 2 == p)
            def _():
                pair_copy(xs, s).wait_send()

            core_copy(xs, s).wait()
            return inner

        lax.fori_loop(0, pc, finish_s, 0)
        return carry

    lax.fori_loop(0, nx, finish_x, 0)

    def finish_q(qs, carry):
        low_pair(qs).wait()

        @pl.when(goes_right(qs))
        def _():
            low_step(qs, low_sr, q + 1).wait_send()

        @pl.when(goes_left(qs))
        def _():
            low_step(qs, low_sl, q - 1).wait_send()

        return carry

    lax.fori_loop(0, nq, finish_q, 0)


def exchange(children, lower_panel, upper_panel, n_row, n_col, pc):
    nx, nq = n_row // 2, n_col // 2
    rows, cols = children.shape
    kc = cols // TILE
    tk = rows // TILE // nx
    kids = children.reshape(tk, nx, TILE, cols)
    low_rows, low_cols = lower_panel.shape
    if low_cols == TILE:
        low_shape = (low_rows, n_col * TILE)
    else:
        low_shape = (n_col, low_rows, low_cols)
    dma = pltpu.SemaphoreType.DMA
    anywhere = pl.BlockSpec(memory_space=pl.ANY)
    recv, low_all, up_all = pl.pallas_call(
        functools.partial(exchange_kernel, nx, nq, kc, pc),
        out_shape=[
            jax.ShapeDtypeStruct((n_row, tk, TILE, pc * TILE), children.dtype),
            jax.ShapeDtypeStruct(low_shape, lower_panel.dtype),
            jax.ShapeDtypeStruct((n_row,) + upper_panel.shape, upper_panel.dtype),
        ],
        in_specs=[anywhere] * 3,
        out_specs=[anywhere] * 3,
        scratch_shapes=[
            dma((kc, nx)), dma((nx, pc)), dma((nx, pc)), dma((nx, pc)), dma((nx, pc)), dma((nx, pc)),
            dma((nx,)), dma((nx,)), dma((nx,)), dma((nx,)),
            dma((nq,)), dma((nq,)), dma((nq,)), dma((nq,)), dma((nq,)),
        ],
        compiler_params=pltpu.CompilerParams(
            collective_id=0, has_side_effects=True, vmem_limit_bytes=4 * 1024 * 1024
        ),
    )(kids, lower_panel, upper_panel)
    if low_cols != TILE:
        low_all = low_all.transpose(1, 0, 2).reshape(low_rows, n_col * low_cols)
    return (
        recv.reshape(2, n_row * tk * TILE // 2, pc * TILE),
        low_all,
        up_all.reshape(-1, pc * TILE),
    )


def front_kernel(band, width, masks, kids, low, up, out):
    first = pl.program_id(0) * band
    for start in range(0, out.shape[1], width):
        cols = pl.ds(start, width)
        product = jnp.dot(low[...], up[:, cols], preferred_element_type=jnp.float32)
        for k in range(band):
            rows = pl.ds(k * TILE, TILE)
            total = kids[0, rows, cols].astype(jnp.float32) * masks[0, pl.ds(first + k, 1), cols]
            total += kids[1, rows, cols].astype(jnp.float32) * masks[1, pl.ds(first + k, 1), cols]
            total -= product[k * TILE:(k + 1) * TILE] * masks[2, pl.ds(first + k, 1), cols]
            out[rows, cols] = total


def build_front(masks, kids, low, up, pr, pc):
    band = next(b for b in (4, 2, 1) if pr % b == 0)
    ncols, depth = pc * TILE, low.shape[1]
    width = next(w for w in (1280, 640, 512, 256, 128) if ncols % w == 0)
    return pl.pallas_call(
        functools.partial(front_kernel, band, width),
        grid=(pr // band,),
        out_shape=jax.ShapeDtypeStruct((pr * TILE, ncols), jnp.float32),
        in_specs=[
            pl.BlockSpec(memory_space=pltpu.VMEM),
            pl.BlockSpec((2, band * TILE, ncols), lambda i: (0, i, 0)),
            pl.BlockSpec((band * TILE, depth), lambda i: (i, 0)),
            pl.BlockSpec(memory_space=pltpu.VMEM),
        ],
        out_specs=pl.BlockSpec((band * TILE, ncols), lambda i: (i, 0)),
        compiler_params=pltpu.CompilerParams(vmem_limit_bytes=56 * 1024 * 1024),
        cost_estimate=pl.CostEstimate(
            flops=2 * pr * TILE * ncols * depth,
            bytes_accessed=8 * pr * TILE * ncols,
            transcendentals=0,
        ),
    )(masks, kids, low, up)


def body(children, row_maps, col_maps, pairs, lower_panel, upper_panel):
    n_row, n_col = lax.axis_size("row"), lax.axis_size("col")
    row, col = lax.axis_index("row"), lax.axis_index("col")
    nx, nq = n_row // 2, n_col // 2
    pr = lower_panel.shape[0] // TILE
    pc = upper_panel.shape[1] // TILE
    row_ids = row * pr + jnp.arange(pr, dtype=jnp.int32)
    col_ids = col * pc + jnp.arange(pc, dtype=jnp.int32)
    mine_rows = lax.dynamic_index_in_dim(row_maps.reshape(2, pr, nx), row // 2, 2, keepdims=False)
    mine_cols = lax.dynamic_index_in_dim(col_maps.reshape(2, pc, nq), col // 2, 2, keepdims=False)
    row_on = (mine_rows == row_ids[None]).astype(jnp.float32)
    col_on = (mine_cols == col_ids[None]).astype(jnp.float32)
    row_hit = (pairs[:, 0][:, None] == row_ids[None]).astype(jnp.bfloat16)
    col_hit = (pairs[:, 1][:, None] == col_ids[None]).astype(jnp.bfloat16)
    listed = jnp.dot(row_hit.T, col_hit, preferred_element_type=jnp.float32)
    masks = jnp.concatenate([row_on[:, :, None] * col_on[:, None, :], listed[None]])
    masks = jnp.repeat(masks, TILE, axis=2)
    kids, low, up = exchange(children, lower_panel, upper_panel, n_row, n_col, pc)
    return build_front(masks, kids, low, up, pr, pc)


def solution(mesh):
    placed = (P("row", "col"), P(), P(), P(), P("row", "col"), P("row", "col"))
    return jax.shard_map(
        body, mesh=mesh, in_specs=placed, out_specs=P("row", "col"), check_vma=False
    )
```

time: 2220 us -> 649 us (0.29)
  waiting for transfers between devices: 1150 us -> 0 us
  local copies, waits for them, and re-layouts: 673 us -> 17.5 us
  Pallas kernels: 0 us -> 630 us
  matrix products: 197 us -> 0.99 us
  other arithmetic: 142 us -> 0.27 us
  starting transfers between devices: 37.6 us -> 0 us
    all_to_all x2 -> x0, waiting for transfers between devices: 1150 us -> none  [the longest x1 664 us: body(): lax.all_to_all(outgoing, 'col', split_axis=1, concat_axis=1, tiled=True)]
    pallas_call x0 -> x2, Pallas kernels: none -> 630 us  [the longest x1 579 us: exchange(): pl.pallas_call(functools.partial(exchange_kernel, nx, nq, kc, pc), out_sh...]
    gather x14 -> x0, local copies, waits for them, and re-layouts: 408 us -> none  [the longest x6 216 us: body(): jnp.take(strip.reshape(row_per, TILE * parent_cols * TILE), row_pick, axi...]
    dot_general x3 -> x0, matrix products: 196 us -> none  [the longest x1 89.6 us: body(): jnp.dot(arrived, col_place, preferred_element_type=jnp.float32)]
    reshape x3, local copies, waits for them, and re-layouts: 108 us -> 4.03 us  [the longest x1 2.48 us: body(): masks = jnp.repeat(masks, TILE, axis=2)]
    mul x2 -> x0, local copies, waits for them, and re-layouts: 70.5 us -> none  [body(): product.reshape(parent_rows, TILE, parent_cols, TILE)]
    add x1 -> x0, local copies, waits for them, and re-layouts: 48.9 us -> none  [body(): assembled + gathered.reshape(parent_rows, TILE, parent_cols, TILE)]
    add x5 -> x2, other arithmetic: 47.9 us -> 0.01 us  [the longest x1 0.01 us: body(): col_ids = col * pc + jnp.arange(pc, dtype=jnp.int32)]
  transfers between devices with their start and end apart: 4 -> 0, of which waited for: 2 -> 0; matrix products, arithmetic and copies ran while one was open for 22% -> 0% of each run, Pallas kernels for 0% -> 0%
where the time goes in v1:
time: 649 us
  Pallas kernels  630 us (97%)
  local copies, waits for them, and re-layouts  17.5 us (3%)
    pallas_call x1, Pallas kernels, exchange(): pl.pallas_call(functools.partial(exchange_kernel, nx, nq, kc, pc), out_sh...  579 us
    pallas_call x1, Pallas kernels, build_front(): pl.pallas_call(functools.partial(front_kernel, band, width), grid=(pr //...  50.9 us

profile of v1, /device:TPU:25, one launch (start us, length us, event | category | flops | bytes accessed | tf_op | source)
XLA Modules:
  0.0 648.7 jit_solution(17057159357681576921)
XLA Ops:
  0.0 0.0 copy-start.4
  0.0 0.0 copy-start.3
  0.0 0.9 fusion.6
  0.9 1.0 convolution_bitcast_fusion
  1.9 0.8 reshape.51
  2.7 0.2 dynamic-slice_reduce_fusion
  2.9 0.8 reshape.50
  3.7 0.2 convert_reduce_fusion
  3.9 0.1 broadcast_multiply_fusion
  4.0 1.6 broadcast_in_dim.5
  5.5 2.5 reshape.52.masks
  8.0 0.0 copy-done.4
  8.0 0.0 copy-done.3
  8.0 0.0 copy-start
  8.0 4.7 copy-done
  12.7 578.9 %shard_map.64 = (bf16[4,20,128,2560]{3,2,1,0:T(8,128)(2,1)}, bf16[5120,1024]{1,0:T(8,128)(2,1)S(1)}, bf16[4,256,2560]{2,1,0:T(8,128)(2,1)S(1)}) custom-call(bf16[20,2,128,1280]{3,2,1,0:T(8,128)(2,1)S(1)} %bitcast.8, bf16[5120,128]{1,0:T(8,128)(2,1)S(1)} %copy-done.3, bf16[256,2560]{1,0:T(8,128)(2,1)S(1)} %copy-done.4), custom_call_target="tpu_custom_call" | custom-call | tf_op jit(solution)/shard_map/pallas_call | solution.py:270
  591.6 0.0 copy-start.1
  591.6 3.9 copy-done.1
  595.5 0.0 copy-start.2
  595.5 2.3 copy-done.2
  597.8 50.9 %shard_map.65 = f32[5120,2560]{1,0:T(8,128)} custom-call(f32[3,40,2560]{2,1,0:T(8,128)} %reshape.52.masks, bf16[2,5120,2560]{2,1,0:T(8,128)(2,1)} %bitcast.10, bf16[5120,1024]{1,0:T(8,128)(2,1)} %copy-done.1, bf16[1024,2560]{1,0:T(8,128)(2,1)} %bitcast.9), custom_call_target="tpu_custom_call" | custom-call | flops 26843545600 | bytes 104857600 | tf_op jit(solution)/shard_map/pallas_call | solution.py:314
  (4 shorter events, 0.0 us)
Async XLA Ops:
  0.0 8.0 %copy-start.4 = (bf16[256,2560]{1,0:T(8,128)(2,1)S(1)}, bf16[256,2560]{1,0:T(8,128)(2,1)}, u32[]{:S(2)}) copy-start(bf16[256,2560]{1,0:T(8,128)(2,1)} %up.1) | copy-start | bytes 3932164
  0.0 8.0 %copy-start.3 = (bf16[5120,128]{1,0:T(8,128)(2,1)S(1)}, bf16[5120,128]{1,0:T(8,128)(2,1)}, u32[]{:S(2)}) copy-start(bf16[5120,128]{1,0:T(8,128)(2,1)} %low.1) | copy-start | bytes 3932164
  8.0 4.7 copy-start
  591.6 3.9 copy-start.1
  595.5 2.3 copy-start.2

commit v2 on v1

--- a/solution.py
+++ b/solution.py
@@ -22,7 +22,7 @@
     recv, low_all, up_all,
     send1, recv1, send2, recv2, send3, recv3,
     up_s1, up_r1, up_s3, up_r3,
-    low_sr, low_sl, low_r1, low_s2, low_r2,
+    low_sr, low_sl, low_sp, low_r,
 ):
     row = lax.axis_index("row")
     col = lax.axis_index("col")
@@ -140,45 +140,64 @@
         ref = up_all.at[2 * xs + core]
         return remote(ref, ref, up_s3.at[xs], up_r3.at[xs], core_mate)
 
-    def low_slot(qs, side):
+    def low_slot(qs, owner):
         if len(low_all.shape) == 3:
-            return low_all.at[2 * qs + side]
-        return low_all.at[:, lanes(2 * qs + side)]
-
-    def low_step(qs, sems, to):
-        ref = low_slot(qs, p)
-        return remote(ref, ref, sems.at[qs], low_r1.at[qs], (row, 2 * to + p))
-
-    def low_pair(qs):
-        ref = low_slot(qs, p)
-        return remote(ref, ref, low_s2.at[qs], low_r2.at[qs], p_mate)
-
-    def goes_right(qs):
-        return (qs <= q) & (q + 1 < nq)
-
-    def goes_left(qs):
-        return (qs >= q) & (q > 0)
-
-    def low_arrived(qs):
-        ref = low_slot(qs, p)
-        pltpu.make_async_copy(ref, ref, low_r1.at[qs]).wait()
-
-        @pl.when(goes_right(qs))
-        def _():
-            low_step(qs, low_sr, q + 1).start()
-
-        @pl.when(goes_left(qs))
-        def _():
-            low_step(qs, low_sl, q - 1).start()
-
-        low_pair(qs).start()
+            return low_all.at[2 * qs + owner]
+        return low_all.at[:, lanes(2 * qs + owner)]
+
+    def low_copy(qs, owner, sems, device):
+        ref = low_slot(qs, owner)
+        k = 2 * qs + owner
+        return remote(ref, ref, sems.at[k], low_r.at[k], device)
+
+    def low_right(qs, owner):
+        return low_copy(qs, owner, low_sr, (row, 2 * (q + 1) + p))
+
+    def low_left(qs, owner):
+        return low_copy(qs, owner, low_sl, (row, 2 * (q - 1) + p))
+
+    def low_pair(qs, owner):
+        return low_copy(qs, owner, low_sp, p_mate)
+
+    def goes_right(qs, owner):
+        return (qs <= q) & (q + 1 < nq) & ((p == 0) | (owner == 1))
+
+    def goes_left(qs, owner):
+        return (qs >= q) & (q > 0) & ((p == 1) | (owner == 0))
+
+    def goes_pair(qs, owner):
+        return (owner == p) & ((qs == q) | ((qs < q) & (p == 0)) | ((qs > q) & (p == 1)))
+
+    def from_pair_only(qs, owner):
+        return (owner != p) & (qs != q) & jnp.logical_not(((qs < q) & (p == 0)) | ((qs > q) & (p == 1)))
+
+    def low_wait(qs, owner):
+        ref = low_slot(qs, owner)
+        pltpu.make_async_copy(ref, ref, low_r.at[2 * qs + owner]).wait()
+
+    def low_arrived(qs, owner):
+        @pl.when(jnp.logical_not(from_pair_only(qs, owner)))
+        def _():
+            low_wait(qs, owner)
+
+            @pl.when(goes_pair(qs, owner))
+            def _():
+                low_pair(qs, owner).start()
+
+            @pl.when(goes_right(qs, owner))
+            def _():
+                low_right(qs, owner).start()
+
+            @pl.when(goes_left(qs, owner))
+            def _():
+                low_left(qs, owner).start()
 
     def up_arrived(xs):
         ref = up_all.at[2 * xs + core]
         pltpu.make_async_copy(ref, ref, up_r1.at[xs]).wait()
         up_core(xs).start()
 
-    pltpu.make_async_copy(low, low_slot(q, p), low_r1.at[q]).start()
+    pltpu.make_async_copy(low, low_slot(q, p), low_r.at[col]).start()
     pltpu.make_async_copy(up, up_all.at[row], up_r1.at[x]).start()
     for dx in range(1, nx):
         up_far(lax.rem(x + dx, nx)).start()
@@ -192,11 +211,13 @@
 
         @pl.when((m < nq) & (q - m >= 0))
         def _():
-            low_arrived(q - m)
+            low_arrived(q - m, p)
+            low_arrived(q - m, 1 - p)
 
         @pl.when((m > 0) & (q + m < nq))
         def _():
-            low_arrived(q + m)
+            low_arrived(q + m, p)
+            low_arrived(q + m, 1 - p)
 
         @pl.when(m < kc)
         def _():
@@ -238,20 +259,28 @@
 
     lax.fori_loop(0, nx, finish_x, 0)
 
-    def finish_q(qs, carry):
-        low_pair(qs).wait()
-
-        @pl.when(goes_right(qs))
-        def _():
-            low_step(qs, low_sr, q + 1).wait_send()
-
-        @pl.when(goes_left(qs))
-        def _():
-            low_step(qs, low_sl, q - 1).wait_send()
+    def finish_low(k, carry):
+        qs, owner = k // 2, k % 2
+
+        @pl.when(from_pair_only(qs, owner))
+        def _():
+            low_wait(qs, owner)
+
+        @pl.when(goes_pair(qs, owner))
+        def _():
+            low_pair(qs, owner).wait_send()
+
+        @pl.when(goes_right(qs, owner))
+        def _():
+            low_right(qs, owner).wait_send()
+
+        @pl.when(goes_left(qs, owner))
+        def _():
+            low_left(qs, owner).wait_send()
 
         return carry
 
-    lax.fori_loop(0, nq, finish_q, 0)
+    lax.fori_loop(0, 2 * nq, finish_low, 0)
 
 
 def exchange(children, lower_panel, upper_panel, n_row, n_col, pc):
@@ -279,10 +308,10 @@
         scratch_shapes=[
             dma((kc, nx)), dma((nx, pc)), dma((nx, pc)), dma((nx, pc)), dma((nx, pc)), dma((nx, pc)),
             dma((nx,)), dma((nx,)), dma((nx,)), dma((nx,)),
-            dma((nq,)), dma((nq,)), dma((nq,)), dma((nq,)), dma((nq,)),
+            dma((n_col,)), dma((n_col,)), dma((n_col,)), dma((n_col,)),
         ],
         compiler_params=pltpu.CompilerParams(
-            collective_id=0, has_side_effects=True, vmem_limit_bytes=4 * 1024 * 1024
+            collective_id=0, has_side_effects=True, vmem_limit_bytes=60 * 1024 * 1024
         ),
     )(kids, lower_panel, upper_panel)
     if low_cols != TILE:

time: 649 us -> 605 us (0.932)
  Pallas kernels: 630 us -> 598 us
  local copies, waits for them, and re-layouts: 17.5 us -> 4.24 us
    pallas_call x1, Pallas kernels: 579 us -> 547 us  [exchange(): pl.pallas_call(functools.partial(exchange_kernel, nx, nq, kc, pc), out_sh...]
    unnamed x10 -> x0, local copies, waits for them, and re-layouts: 10.9 us -> none
where the time goes in v2:
time: 605 us; the launch traced here: 603 us
  Pallas kernels  598 us (99%)
    pallas_call x1, Pallas kernels, exchange(): pl.pallas_call(functools.partial(exchange_kernel, nx, nq, kc, pc), out_sh...  547 us
    pallas_call x1, Pallas kernels, build_front(): pl.pallas_call(functools.partial(front_kernel, band, width), grid=(pr //...  51 us

profile of v2, /device:TPU:25, one launch (start us, length us, event | category | flops | bytes accessed | tf_op | source)
XLA Modules:
  0.0 603.2 jit_solution(6525138508649803339)
XLA Ops:
  0.0 0.8 fusion.6
  0.8 1.0 convolution_bitcast_fusion
  1.8 0.8 reshape.51
  2.6 0.2 dynamic-slice_reduce_fusion
  2.8 0.8 reshape.50
  3.6 0.2 convert_reduce_fusion
  3.8 0.1 broadcast_multiply_fusion
  3.9 0.4 broadcast_in_dim.5
  4.3 1.2 reshape.52.masks
  5.5 546.6 %shard_map.64 = (bf16[4,20,128,2560]{3,2,1,0:T(8,128)(2,1)}, bf16[5120,1024]{1,0:T(8,128)(2,1)}, bf16[4,256,2560]{2,1,0:T(8,128)(2,1)}) custom-call(bf16[20,2,128,1280]{3,2,1,0:T(8,128)(2,1)} %bitcast.9, bf16[5120,128]{1,0:T(8,128)(2,1)} %low.1, bf16[256,2560]{1,0:T(8,128)(2,1)} %up.1), custom_call_target="tpu_custom_call" | custom-call | tf_op jit(solution)/shard_map/pallas_call | solution.py:299
  552.2 51.0 %shard_map.65 = f32[5120,2560]{1,0:T(8,128)} custom-call(f32[3,40,2560]{2,1,0:T(8,128)} %reshape.52.masks, bf16[2,5120,2560]{2,1,0:T(8,128)(2,1)} %bitcast.8, bf16[5120,1024]{1,0:T(8,128)(2,1)} %get-tuple-element.9.low, bf16[1024,2560]{1,0:T(8,128)(2,1)} %bitcast.10), custom_call_target="tpu_custom_call" | custom-call | flops 26843545600 | bytes 104857600 | tf_op jit(solution)/shard_map/pallas_call | solution.py:343
  (4 shorter events, 0.0 us)
